TPU v7x, 32 devices: a whole 2x2x4 slice. The times are simulated.
32 devices in a mesh: gx: 2 (over y), gy: 16 (over z, x, core).
Axes of the slice: x: 2, y: 2, z: 4, core: 2. Of those that a mesh axis runs over, the one named last changes fastest.
Arguments:
- source: float32 [128, 64, 128], P('gy', 'gx'), may hold values from -0.004 to 0.004
- mask: int32 [128, 64, 128], P('gy', 'gx'), may hold values from 0 to 2, as said below
- cond_x: float32 [128, 64, 128], P('gy', 'gx'), may hold values from 0.0012 to 0.06
- cond_y: float32 [128, 64, 128], P('gy', 'gx'), may hold values from 0.4 to 5
- cond_z: float32 [128, 64, 128], P('gy', 'gx'), may hold values from 0.0004 to 0.01
Outputs:
- solution: float32 [128, 64, 128], P('gy', 'gx')
Inputs may be any that keep to these rules, and one draw needn't show every extreme that they name: `mask`: 0 marks a fluid cell, 1 a cut cell, 2 a solid cell.
All inputs are finite; a program needn't handle non-finite values.
Results may differ from a plain program's by a relative error of at most 0.00095.
Values sent between devices are 32-bit elements; how exact they have to be, the bound alone decides.
A program may use at most 128 MiB of HBM per device.

v0:
```python
import jax
import jax.numpy as jnp
from jax import lax
from jax.sharding import PartitionSpec as P

LEVELS = 6


base_shift = 0.001
wall_term = 0.02


def padded(cells, sides, width):
    for axis, dim in sides:
        count = lax.axis_size(axis)
        ends = count - 1
        head = lax.slice_in_dim(cells, 0, width, axis=dim)
        tail = lax.slice_in_dim(cells, cells.shape[dim] - width, cells.shape[dim], axis=dim)
        cells = jnp.concatenate(
            [
                lax.ppermute(tail, axis, [(i, (i + 1) % count) for i in range(ends)]),
                cells,
                lax.ppermute(head, axis, [((i + 1) % count, i) for i in range(ends)]),
            ],
            axis=dim,
        )
    return cells


def swapped(x, axis, stride):
    return lax.ppermute(x, axis, [(i, i ^ 1 << stride) for i in range(lax.axis_size(axis))])


def ahead(field, axis):
    size = field.shape[axis]
    edge = jnp.zeros_like(lax.slice_in_dim(field, 0, 1, axis=axis))
    return jnp.concatenate([lax.slice_in_dim(field, 1, size, axis=axis), edge], axis=axis)


def behind(field, axis):
    size = field.shape[axis]
    edge = jnp.zeros_like(lax.slice_in_dim(field, 0, 1, axis=axis))
    return jnp.concatenate([edge, lax.slice_in_dim(field, 0, size - 1, axis=axis)], axis=axis)


def coarse_sum(field):
    depth, width, height = field.shape
    return field.reshape(depth // 2, 2, width // 2, 2, height // 2, 2).sum(axis=(1, 3, 5))


def coarse_face(face, axis, parity):
    picked = lax.slice_in_dim(face, parity, face.shape[axis], stride=2, axis=axis)
    return 0.125 * coarse_sum(jnp.repeat(picked, 2, axis=axis))


def prolong(field):
    return jnp.repeat(jnp.repeat(jnp.repeat(field, 2, axis=0), 2, axis=1), 2, axis=2)


def upper_flag(bit):
    return lax.axis_index("gy") // 2**bit % 2


def line_factors(lower, diag, upper):
    denoms = [diag[0]]
    ratios = [upper[0] / diag[0]]
    for place in range(1, diag.shape[0]):
        pivot = diag[place] - lower[place] * ratios[place - 1]
        denoms.append(pivot)
        ratios.append(upper[place] / pivot)
    return (denoms, ratios)


def rows_solve(level, rhs):
    lower = level["lower"]
    denoms = level["denoms"]
    ratios = level["ratios"]
    count = rhs.shape[0]
    values = [rhs[0] / denoms[0]]
    for place in range(1, count):
        values.append((rhs[place] - lower[place] * values[place - 1]) / denoms[place])
    result = [values[count - 1]]
    for place in range(count - 2, -1, -1):
        result.append(values[place] - ratios[place] * result[-1])
    return jnp.stack(result[::-1])


def assemble(faces, group):
    face_x, low_x, face_y, low_y, face_z, shift = faces
    low_z = behind(face_z, 2)
    diag = shift + face_x + low_x + face_y + low_y + face_z + low_z
    level = {
        "face_x": face_x,
        "low_x": low_x,
        "face_y": face_y,
        "low_y": low_y,
        "face_z": face_z,
        "low_z": low_z,
        "diag": diag,
        "group": group,
    }
    level["lower"] = -low_y
    denoms, ratios = line_factors(-low_y, diag, -face_y)
    level["denoms"] = denoms
    level["ratios"] = ratios
    blank = jnp.zeros_like(diag)
    level["first_resp"] = rows_solve(level, blank.at[0].set(1.0))
    level["last_resp"] = rows_solve(level, blank.at[-1].set(1.0))
    level["alpha"] = low_y[0] * level["first_resp"][0]
    level["gamma"] = low_y[0] * level["first_resp"][-1]
    level["beta"] = face_y[-1] * level["last_resp"][0]
    level["delta"] = face_y[-1] * level["last_resp"][-1]
    return level


def forward_terms(alpha, beta, gamma, delta, head, tail):
    zeros = jnp.zeros_like(head)
    ones = jnp.ones_like(head)
    return (
        gamma * beta - alpha * delta,
        zeros,
        delta,
        gamma * head - alpha * tail,
        gamma,
        tail,
        -alpha,
        zeros,
        ones,
    )


def chain_forward(earlier, later):
    product = []
    for left_row in range(3):
        for column in range(3):
            product.append(
                later[3 * left_row] * earlier[column]
                + later[3 * left_row + 1] * earlier[3 + column]
                + later[3 * left_row + 2] * earlier[6 + column]
            )
    scale = product[8]
    return tuple((entry / scale for entry in product))


def chain_backward(earlier, later):
    return (later[0] + later[1] * earlier[0], later[1] * earlier[1])


def settle(alpha, beta, head, state):
    carry_q = state[2] / state[8]
    carry_p = state[5] / state[8]
    pivot = 1.0 - alpha * carry_q
    return ((head + alpha * carry_p) / pivot, beta / pivot, carry_q, carry_p)


def reduced_local(alpha, beta, gamma, delta, head, tail):
    zeros = jnp.zeros_like(head[:1])
    ones = jnp.ones_like(head[:1])
    identity = (ones, zeros, zeros, zeros, ones, zeros, zeros, zeros, ones)
    terms = forward_terms(alpha, beta, gamma, delta, head, tail)
    inclusive = lax.associative_scan(chain_forward, terms, axis=0)
    state = tuple(
        (jnp.concatenate([plain, entry[:-1]], axis=0) for plain, entry in zip(identity, inclusive))
    )
    start, slope, carry_q, carry_p = settle(alpha, beta, head, state)
    later = lax.associative_scan(chain_backward, (start, slope), reverse=True, axis=0)
    next_first = jnp.concatenate([later[0][1:], zeros], axis=0)
    first = start + slope * next_first
    return (carry_p + carry_q * first, next_first)


def pick_block(values, index, shape):
    return lax.dynamic_index_in_dim(values, index, 0, keepdims=False).reshape(shape)


def reduced_moved(level, head, tail):
    group = level["group"]
    shape = head.shape
    packed = jnp.stack(
        [level["alpha"], level["beta"], level["gamma"], level["delta"], head, tail]
    ).reshape(6, 1, -1)
    if group == 1:
        moved = lax.all_to_all(packed, "gy", split_axis=2, concat_axis=1, tiled=True)
        prev_last, next_first = reduced_local(
            moved[0], moved[1], moved[2], moved[3], moved[4], moved[5]
        )
        back = lax.all_to_all(
            jnp.stack([prev_last, next_first]), "gy", split_axis=1, concat_axis=2, tiled=True
        )
        return (back[0, 0].reshape(shape), back[1, 0].reshape(shape))
    whole = lax.all_gather(packed, "gy", axis=1, tiled=True)
    whole = whole.reshape(6, whole.shape[1] // group, group, -1)[:, :, 0]
    prev_last, next_first = reduced_local(
        whole[0], whole[1], whole[2], whole[3], whole[4], whole[5]
    )
    index = lax.axis_index("gy") // group
    return (pick_block(prev_last, index, shape), pick_block(next_first, index, shape))


def line_solve(level, rhs):
    local = rows_solve(level, rhs)
    prev_last, next_first = reduced_moved(level, local[0], local[-1])
    return (
        local
        + (level["low_y"][0] * prev_last)[None] * level["first_resp"]
        + (level["face_y"][-1] * next_first)[None] * level["last_resp"]
    )


def neighbour_terms(level, field):
    rim = padded(field, (("gx", 1),), 1)
    return (
        level["face_x"] * rim[:, 2:]
        + level["low_x"] * rim[:, :-2]
        + level["face_z"] * ahead(field, 2)
        + level["low_z"] * behind(field, 2)
    )


def relax(level, field, rhs):
    return line_solve(level, rhs + neighbour_terms(level, field))


def body(source, mask, cond_x, cond_y, cond_z):
    open_cells = (mask != 2).astype(jnp.float32)
    wall = (mask == 1).astype(jnp.float32)
    rim = padded(
        jnp.stack([cond_x * open_cells, cond_y * open_cells, open_cells]), (("gx", 2), ("gy", 1)), 1
    )
    faces = (
        cond_x * open_cells * rim[2, 1:-1, 2:],
        rim[0, 1:-1, :-2] * open_cells,
        cond_y * open_cells * rim[2, 2:, 1:-1],
        rim[1, :-2, 1:-1] * open_cells,
        cond_z * open_cells * ahead(open_cells, 2),
        base_shift + wall_term * wall,
    )
    rhs = source * open_cells
    levels = []
    fields = []
    sources = []
    residual = rhs
    for depth in range(LEVELS):
        group = 1
        if depth > 0:
            face_x, low_x, face_y, low_y, face_z, shift = faces
            faces = (
                coarse_face(face_x, 1, 1),
                coarse_face(low_x, 1, 0),
                coarse_face(face_y, 0, 1),
                coarse_face(low_y, 0, 0),
                coarse_face(face_z, 2, 1),
                0.25 * coarse_sum(shift),
            )
            rhs = 0.25 * coarse_sum(residual)
            if depth >= 2:
                group = 2 ** (depth - 1)
                stacked = jnp.stack((rhs,) + faces)
                partner = swapped(stacked, "gy", depth - 2)
                upper = upper_flag(depth - 2) == 1
                folded = jnp.concatenate(
                    [jnp.where(upper, partner, stacked), jnp.where(upper, stacked, partner)], axis=1
                )
                rhs = folded[0]
                faces = tuple((folded[place] for place in range(1, 7)))
        level = assemble(faces, group)
        field = line_solve(level, rhs)
        if depth == LEVELS - 1:
            field = relax(level, field, rhs)
        else:
            residual = neighbour_terms(level, field)
        levels.append(level)
        fields.append(field)
        sources.append(rhs)
    correction = fields[-1]
    for depth in range(LEVELS - 2, -1, -1):
        if depth + 1 >= 2:
            half = correction.shape[0] // 2
            correction = lax.dynamic_slice_in_dim(correction, upper_flag(depth - 1) * half, half, 0)
        field = fields[depth] + prolong(correction)
        correction = relax(levels[depth], field, sources[depth])
    return correction


def solution(mesh):
    return jax.shard_map(
        body,
        mesh=mesh,
        in_specs=(
            P("gy", "gx", None),
            P("gy", "gx", None),
            P("gy", "gx", None),
            P("gy", "gx", None),
            P("gy", "gx", None),
        ),
        out_specs=P("gy", "gx", None),
        check_vma=False,
    )
```

profile of v0, /device:TPU:0, one launch (start us, length us, event | category | flops | bytes accessed | tf_op | source)
XLA Modules:
  0.0 828.7 jit_solution(11314985049572745584)
XLA Ops:
  3.4 4.9 collective-permute-start.1
  11.1 9.8 %reshape.2407 = f32[4,2,16,2,64,2]{5,4,3,2,1,0:T(8,128)} reshape(f32[8,32,128]{2,1,0:T(8,128)S(1)} %get-tuple-element.552) | data formatting | bytes 262144 | tf_op jit(solution)/shard_map/reshape | solution.py:48
  20.9 4.7 reduce_sum.331
  26.9 4.6 collective-permute-done.2
  41.8 19.2 %reduce.147 = f32[4096,6]{1,0:T(8,128)} reduce(f32[4096,1,6]{2,1,0:T(1,128)S(1)} %bitcast.847, f32[]{:T(128)} %broadcast.1790), dimensions={1}, to_apply=%bitcast.767.reduce_sub_computation | reduce | bytes 196612
  65.4 8.7 %all-to-all-start = ((f32[16,1,1536]{2,1,0:T(1,128)}), f32[16,1,1536]{2,1,0:T(1,128)}, u32[]{:S(2)}, u32[]{:S(2)}) async-start(f32[16,1,1536]{2,1,0:T(1,128)} %reshape.2551), calls=%async_computation | async-start | bytes 196608 | tf_op jit(solution)/shard_map/all_to_all | solution.py:183
  106.5 70.1 %slice_reduce_fusion.6 = (f32[4096]{0:T(1024)}, f32[4096]{0:T(1024)}, f32[4096]{0:T(1024)}, f32[4096]{0:T(1024)}, f32[4096]{0:T(1024)}, /*index=5*/f32[4096]{0:T(1024)}, f32[1,1,4096]{0,1,2:T(1,128)}) fusion(f32[6,1,4096]{0,1,2:T(1,128)S(1)} %bitcast.839), kind=kLoop, calls=%fused_computation.6 | loop fusion | bytes 212992 | tf_op jit(solution)/shard_map/slice | solution.py:185
  304.0 6.1 all-to-all-start.1
  310.1 6.6 all-to-all-done.1
  318.1 4.5 collective-permute-start.5
  324.2 20.8 %reshape.2406 = f32[4,2,16,2,64,2]{5,4,3,2,1,0:T(8,128)} reshape(f32[8,32,128]{2,1,0:T(8,128)S(1)} %fusion.9) | data formatting | bytes 262144 | tf_op jit(solution)/shard_map/reshape | solution.py:48
  357.6 6.2 all-to-all-done.2
  365.2 17.1 %slice_reduce_fusion.16 = (f32[1024]{0:T(1024)S(1)}, f32[1024]{0:T(1024)S(1)}, f32[1024]{0:T(1024)S(1)}, f32[1024]{0:T(1024)S(1)}, f32[1024]{0:T(1024)S(1)}, /*index=5*/f32[1024]{0:T(1024)S(1)}, f32[1,1,1024]{0,1,2:T(1,128)S(1)}) fusion(f32[6,1,1024]{0,1,2:T(1,128)S(1)} %bitcast.843), kind=kLoop, calls=%fused_computation.16 | loop fusion | bytes 53248 | tf_op jit(solution)/shard_map/slice | solution.py:185
  392.1 5.0 all-to-all-done.3
  399.2 4.9 collective-permute-start.7
  408.5 17.9 %all_gather.24 = f32[6,16,256]{2,0,1:T(8,128)S(1)} all-gather(f32[6,1,256]{2,0,1:T(8,128)S(1)} %copy.528), channel_id=1, replica_groups=mesh['gx'=2,'gy'=16] {'gy'}, dimensions={1}, use_global_device_ids=true | all-gather | bytes 104448 | tf_op jit(solution)/shard_map/all_gather | solution.py:191
  444.3 18.8 %all_gather.25 = f32[6,16,64]{2,0,1:T(8,128)S(1)} all-gather(f32[6,1,64]{2,0,1:T(8,128)S(1)} %copy.543), channel_id=1, replica_groups=mesh['gx'=2,'gy'=16] {'gy'}, dimensions={1}, use_global_device_ids=true | all-gather | bytes 26112 | tf_op jit(solution)/shard_map/all_gather | solution.py:191
  476.7 17.8 %all_gather.26 = f32[6,16,16]{2,0,1:T(8,128)S(1)} all-gather(f32[6,1,16]{2,0,1:T(8,128)S(1)} %copy.554), channel_id=1, replica_groups=mesh['gx'=2,'gy'=16] {'gy'}, dimensions={1}, use_global_device_ids=true | all-gather | bytes 6528 | tf_op jit(solution)/shard_map/all_gather | solution.py:191
  507.8 18.7 %all_gather.27 = f32[6,16,4]{0,2,1:T(4,128)S(1)} all-gather(f32[6,1,4]{0,2,1:T(4,128)S(1)} %copy.578), channel_id=1, replica_groups=mesh['gx'=2,'gy'=16] {'gy'}, dimensions={1}, use_global_device_ids=true | all-gather | bytes 1632 | tf_op jit(solution)/shard_map/all_gather | solution.py:191
  534.1 17.7 %all_gather.28 = f32[6,16,4]{0,2,1:T(4,128)S(1)} all-gather(f32[6,1,4]{0,2,1:T(4,128)S(1)} %copy.580), channel_id=1, replica_groups=mesh['gx'=2,'gy'=16] {'gy'}, dimensions={1}, use_global_device_ids=true | all-gather | bytes 1632 | tf_op jit(solution)/shard_map/all_gather | solution.py:191
  559.6 18.8 %all_gather.29 = f32[6,16,16]{2,0,1:T(8,128)S(1)} all-gather(f32[6,1,16]{2,0,1:T(8,128)S(1)} %copy.584), channel_id=1, replica_groups=mesh['gx'=2,'gy'=16] {'gy'}, dimensions={1}, use_global_device_ids=true | all-gather | bytes 6528 | tf_op jit(solution)/shard_map/all_gather | solution.py:191
  580.5 4.5 collective-permute-start.23
  586.7 17.8 %all_gather.30 = f32[6,16,64]{2,0,1:T(8,128)S(1)} all-gather(f32[6,1,64]{2,0,1:T(8,128)S(1)} %copy.598), channel_id=1, replica_groups=mesh['gx'=2,'gy'=16] {'gy'}, dimensions={1}, use_global_device_ids=true | all-gather | bytes 26112 | tf_op jit(solution)/shard_map/all_gather | solution.py:191
  613.5 18.9 %all_gather.31 = f32[6,16,256]{2,0,1:T(8,128)S(1)} all-gather(f32[6,1,256]{2,0,1:T(8,128)S(1)} %copy.608), channel_id=1, replica_groups=mesh['gx'=2,'gy'=16] {'gy'}, dimensions={1}, use_global_device_ids=true | all-gather | bytes 104448 | tf_op jit(solution)/shard_map/all_gather | solution.py:191
  645.6 9.3 %all_to_all.32 = f32[16,1,384]{2,1,0:T(1,128)S(1)} all-to-all(f32[16,1,384]{2,1,0:T(1,128)S(1)} %reshape.2557), channel_id=1, replica_groups=mesh['gx'=2,'gy'=16] {'gy'}, dimensions={0} | all-to-all | bytes 49152 | tf_op jit(solution)/shard_map/all_to_all | solution.py:183
  656.4 17.1 %slice_reduce_fusion.11 = (f32[1024]{0:T(1024)S(1)}, f32[1024]{0:T(1024)S(1)}, f32[1024]{0:T(1024)S(1)}, f32[1024]{0:T(1024)S(1)}, f32[1024]{0:T(1024)S(1)}, /*index=5*/f32[1024]{0:T(1024)S(1)}, f32[1,1,1024]{0,1,2:T(1,128)S(1)}) fusion(f32[6,1,1024]{0,1,2:T(1,128)S(1)} %bitcast.845), kind=kLoop, calls=%fused_computation.11 | loop fusion | bytes 53248 | tf_op jit(solution)/shard_map/slice | solution.py:185
  677.8 9.0 %all_to_all.33 = f32[16,1,128]{2,1,0:T(1,128)S(1)} all-to-all(f32[16,1,128]{2,1,0:T(1,128)S(1)} %reshape.2559), channel_id=1, replica_groups=mesh['gx'=2,'gy'=16] {'gy'}, dimensions={0} | all-to-all | bytes 16384 | tf_op jit(solution)/shard_map/all_to_all | solution.py:187
  689.5 4.8 collective-permute-start.29
  701.0 19.2 %reduce.155 = f32[4096,6]{1,0:T(8,128)} reduce(f32[4096,1,6]{2,1,0:T(1,128)S(1)} %bitcast.850, f32[]{:T(128)} %broadcast.1790), dimensions={1}, to_apply=%bitcast.777.reduce_sub_computation | reduce | bytes 196612
  728.1 7.3 all-to-all-done.6
  739.3 69.5 %slice_reduce_fusion.1 = (f32[4096]{0:T(1024)S(1)}, f32[4096]{0:T(1024)S(1)}, f32[4096]{0:T(1024)S(1)}, f32[4096]{0:T(1024)S(1)}, f32[4096]{0:T(1024)S(1)}, /*index=5*/f32[4096]{0:T(1024)S(1)}, f32[1,1,4096]{0,1,2:T(1,128)}) fusion(f32[6,1,4096]{0,1,2:T(1,128)S(1)} %bitcast.841), kind=kLoop, calls=%fused_computation.1 | loop fusion | bytes 212992 | tf_op jit(solution)/shard_map/slice | solution.py:185
  820.9 6.6 all-to-all-done.7
  (1800 shorter events, 335.6 us)
Async XLA Ops:
  2.1 6.2 collective-permute-start
  3.4 6.3 collective-permute-start.1
  9.7 17.2 %collective-permute-start.3 = (f32[3,1,34,128]{3,2,1,0:T(8,128)S(1)}, f32[3,1,34,128]{3,2,1,0:T(8,128)S(1)}, u32[]{:S(2)}, u32[]{:S(2)}) collective-permute-start(f32[3,1,34,128]{3,2,1,0:T(8,128)S(1)} %get-tuple-element.523), channel_id=1, source_target_pairs={{0,1},{1,2},{2,3},{3,4},{4,5},{5,6},{6,7},{7,8},{8,9},{9,10},{10,1... | collective-permute-start | bytes 156680 | tf_op jit(solution)/shard_map/ppermute | solution.py:21
  25.6 6.0 collective-permute-start.2
  65.4 34.8 %all-to-all-start = ((f32[16,1,1536]{2,1,0:T(1,128)}), f32[16,1,1536]{2,1,0:T(1,128)}, u32[]{:S(2)}, u32[]{:S(2)}) async-start(f32[16,1,1536]{2,1,0:T(1,128)} %reshape.2551), calls=%async_computation | async-start | bytes 196608 | tf_op jit(solution)/shard_map/all_to_all | solution.py:183
  304.0 12.7 %all-to-all-start.1 = ((f32[2,16,256]{2,0,1:T(2,128)}), f32[2,16,256]{2,0,1:T(2,128)S(1)}, u32[]{:S(2)}, u32[]{:S(2)}) async-start(f32[2,16,256]{2,0,1:T(2,128)} %copy.506), calls=%async_computation.1 | async-start | bytes 65536 | tf_op jit(solution)/shard_map/all_to_all | solution.py:187
  316.8 6.0 collective-permute-start.4
  318.1 5.9 collective-permute-start.5
  353.7 10.0 %all-to-all-start.2 = ((f32[16,1,384]{2,1,0:T(1,128)}), f32[16,1,384]{2,1,0:T(1,128)S(1)}, u32[]{:S(2)}, u32[]{:S(2)}) async-start(f32[16,1,384]{2,1,0:T(1,128)} %reshape.2553), calls=%async_computation.2 | async-start | bytes 49152 | tf_op jit(solution)/shard_map/all_to_all | solution.py:183
  387.3 9.8 %all-to-all-start.3 = ((f32[16,1,128]{2,1,0:T(1,128)}), f32[16,1,128]{2,1,0:T(1,128)S(1)}, u32[]{:S(2)}, u32[]{:S(2)}) async-start(f32[16,1,128]{2,1,0:T(1,128)} %reshape.2555), calls=%async_computation.3 | async-start | bytes 16384 | tf_op jit(solution)/shard_map/all_to_all | solution.py:187
  397.9 6.3 collective-permute-start.6
  399.2 5.8 collective-permute-start.7
  429.5 7.0 collective-permute-start.10
  433.7 5.5 collective-permute-start.9
  464.6 7.1 collective-permute-start.12
  465.9 5.8 collective-permute-start.13
  495.3 6.7 collective-permute-start.15
  496.6 5.8 collective-permute-start.16
  526.7 5.9 collective-permute-start.18
  528.0 5.8 collective-permute-start.19
  552.2 5.9 collective-permute-start.20
  553.5 5.8 collective-permute-start.21
  579.2 5.9 collective-permute-start.22
  580.5 5.8 collective-permute-start.23
  606.0 5.9 collective-permute-start.24
  607.3 5.8 collective-permute-start.25
  635.5 5.9 collective-permute-start.26
  636.8 5.8 collective-permute-start.27
  688.2 6.2 collective-permute-start.28
  689.5 5.9 collective-permute-start.29
  724.2 11.1 %all-to-all-start.6 = ((f32[16,1,1536]{2,1,0:T(1,128)}), f32[16,1,1536]{2,1,0:T(1,128)S(1)}, u32[]{:S(2)}, u32[]{:S(2)}) async-start(f32[16,1,1536]{2,1,0:T(1,128)} %reshape.2561), calls=%async_computation.6 | async-start | bytes 196608 | tf_op jit(solution)/shard_map/all_to_all | solution.py:183
  817.4 10.1 %all-to-all-start.7 = ((f32[2,16,256]{2,0,1:T(2,128)}), f32[2,16,256]{2,0,1:T(2,128)S(1)}, u32[]{:S(2)}, u32[]{:S(2)}) async-start(f32[2,16,256]{2,0,1:T(2,128)} %copy.628), calls=%async_computation.7 | async-start | bytes 65536 | tf_op jit(solution)/shard_map/all_to_all | solution.py:187
  (100 other events, 1279.3 us)
where the time goes:
time: 844 us; the launch traced here: 829 us
  local copies, waits for them, and re-layouts  389 us (46%)
  blocking collectives  165 us (20%)
  starting transfers between devices  104 us (12%)
  other arithmetic  103 us (12%)
  waiting for transfers between devices  61.6 us (7%)
    slice x4, local copies, waits for them, and re-layouts, reduced_moved(): moved[1]  174 us
    all_gather x8, blocking collectives, reduced_moved(): whole = lax.all_gather(packed, 'gy', axis=1, tiled=True)  146 us
    slice x382, local copies, waits for them, and re-layouts, reduced_local(): inclusive = lax.associative_scan(chain_forward, terms, axis=0)  105 us
    ppermute x13, starting transfers between devices, padded(): lax.ppermute(tail, axis, [(i, (i + 1) % count) for i in range(ends)])  56.4 us
    unnamed x37, other arithmetic  47.2 us
    reshape x5, local copies, waits for them, and re-layouts, coarse_sum(): field.reshape(depth // 2, 2, width // 2, 2, height // 2, 2)  32 us
    unnamed x286, local copies, waits for them, and re-layouts  25.2 us
    all_to_all x3, waiting for transfers between devices, reduced_moved(): lax.all_to_all(jnp.stack([prev_last, next_first]), 'gy', split_axis=1, co...  18.2 us
  transfers between devices with their start and end apart: 36, of which 22 were waited for; matrix products, arithmetic and copies ran while one was open for 5% of the time, Pallas kernels for 0%

commit v1 on v0

--- a/solution.py
+++ b/solution.py
@@ -1,6 +1,10 @@
+import functools
+
 import jax
 import jax.numpy as jnp
 from jax import lax
+from jax.experimental import pallas as pl
+from jax.experimental.pallas import tpu as pltpu
 from jax.sharding import PartitionSpec as P
 
 LEVELS = 6
@@ -281,18 +285,617 @@
         correction = relax(levels[depth], field, sources[depth])
     return correction
 
+MESH = pl.DeviceIdType.MESH
+LANES = 128
+EXACT = lax.Precision.HIGHEST
+
+
+def looped(count, step, carry, unroll=4):
+    while count % unroll:
+        unroll //= 2
+
+    def several(outer, carry):
+        for inner in range(unroll):
+            carry = step(outer * unroll + inner, carry)
+        return carry
+
+    return lax.fori_loop(0, count // unroll, several, carry)
+
+
+def pairing(parity):
+    fine = lax.broadcasted_iota(jnp.int32, (LANES, LANES), 0)
+    coarse = lax.broadcasted_iota(jnp.int32, (LANES, LANES), 1)
+    if parity is None:
+        hit = (fine == 2 * coarse) | (fine == 2 * coarse + 1)
+    else:
+        hit = fine == 2 * coarse + parity
+    return jnp.where(hit, 1.0, 0.0).astype(jnp.float32)
+
+
+def spreading():
+    coarse = lax.broadcasted_iota(jnp.int32, (LANES, LANES), 0)
+    fine = lax.broadcasted_iota(jnp.int32, (LANES, LANES), 1)
+    hit = (fine == 2 * coarse) | (fine == 2 * coarse + 1)
+    return jnp.where(hit, 1.0, 0.0).astype(jnp.float32)
+
+
+def times(left, right):
+    return jnp.dot(left, right, precision=EXACT, preferred_element_type=jnp.float32)
+
+
+def coarsened(field, work, y_odd=False, x_odd=False, z_odd=False):
+    rows, wide, lanes = field.shape
+    pairs = field.reshape(rows // 2, 2, wide, lanes)
+    summed = pairs[:, 1] if y_odd else pairs[:, 0] + pairs[:, 1]
+    count = rows // 2 * wide
+    work[pl.ds(0, count), :] = times(summed.reshape(count, lanes), pairing(1 if z_odd else None))
+    result = work[pl.ds(1, count // 2, stride=2), :]
+    if not x_odd:
+        result = result + work[pl.ds(0, count // 2, stride=2), :]
+    return 0.25 * result
+
+
+def put_rows(target, flat, rows):
+    wide = flat.shape[0] // rows
+    if wide % 8 == 0:
+        target[...] = flat.reshape(rows, wide, LANES)
+        return
+    target[...] = jnp.zeros_like(target)
+    for row in range(rows):
+        target[row, pl.ds(0, wide), :] = flat[row * wide : (row + 1) * wide]
+
+
+def spread_add(target, coarse, wide, work):
+    rows = coarse.shape[0]
+    half = coarse.shape[1]
+    flat = times(coarse.reshape(rows * half, LANES), spreading())
+    work[pl.ds(0, rows * half, stride=2), :] = flat
+    work[pl.ds(1, rows * half, stride=2), :] = flat
+    for row in range(rows):
+        extra = work[pl.ds(row * 2 * half, wide), :]
+        target[2 * row] = target[2 * row] + extra
+        target[2 * row + 1] = target[2 * row + 1] + extra
+
+
+class Coarse:
+    names = ("fx", "lx", "fy", "ly", "fz", "lz", "sh", "rec", "u", "g")
+
+    def __init__(self, rows, width, height):
+        self.rows = rows
+        self.width = width
+        self.height = height
+        self.wide = max(8, width)
+
+    def scratch(self):
+        return [pltpu.VMEM((self.rows, self.wide, LANES), jnp.float32)] * len(self.names)
+
+    def bind(self, refs):
+        for name, ref in zip(self.names, refs):
+            setattr(self, name, ref)
+        self.halo = None
+
+    def factor(self, edge=None):
+        row = lax.broadcasted_iota(jnp.int32, (self.wide, LANES), 0)
+        lane = lax.broadcasted_iota(jnp.int32, (self.wide, LANES), 1)
+        blank = jnp.where((row >= self.width) | (lane >= self.height), 1.0, 0.0)
+        zero = jnp.zeros((self.wide, LANES), jnp.float32)
+
+        def step(y, carry):
+            ratio, below = carry
+            fx, fy, fz = self.fx[y], self.fy[y], self.fz[y]
+            lx = pltpu.roll(fx, 1, 0)
+            if edge is not None:
+                lx = jnp.where(row == 0, edge(y), lx)
+            lz = pltpu.roll(fz, 1, 1)
+            diag = self.sh[y] + blank + fx + lx + fy + below + fz + lz
+            rec = 1.0 / (diag - below * ratio)
+            self.lx[y] = lx
+            self.ly[y] = below * rec
+            self.lz[y] = lz
+            self.rec[y] = rec
+            ratio = fy * rec
+            self.sh[y] = ratio
+            return ratio, fy
+
+        looped(self.rows, step, (zero, zero))
+
+    def beside(self, y):
+        u = self.u[y]
+        after = pltpu.roll(u, self.wide - 1, 0)
+        before = pltpu.roll(u, 1, 0)
+        if self.halo is not None:
+            row = lax.broadcasted_iota(jnp.int32, (self.wide, LANES), 0)
+            before = jnp.where(row == 0, self.halo[0, pl.ds(y, 1), :], before)
+            after = jnp.where(row == self.wide - 1, self.halo[1, pl.ds(y, 1), :], after)
+        return (
+            self.fx[y] * after
+            + self.lx[y] * before
+            + self.fz[y] * pltpu.roll(u, LANES - 1, 1)
+            + self.lz[y] * pltpu.roll(u, 1, 1)
+        )
+
+    def solve(self, again):
+        zero = jnp.zeros((self.wide, LANES), jnp.float32)
+
+        def down(y, carry):
+            right = self.g[y]
+            if again:
+                right = right + self.beside(y)
+            value = right * self.rec[y] + self.ly[y] * carry
+            self.u[y] = value
+            return value
+
+        def up(step, carry):
+            y = self.rows - 1 - step
+            value = self.u[y] + self.sh[y] * carry
+            self.u[y] = value
+            return value
+
+        looped(self.rows, down, zero, 8)
+        looped(self.rows, up, zero, 8)
+
+    def residual(self, hold):
+        def step(y, carry):
+            hold[y] = self.beside(y)
+            return carry
+
+        looped(self.rows, step, 0)
+
+
+def v_cycle_kernel(ngx, ngy, levels, *refs):
+    source, mask, cond_x, cond_y, cond_z, out = refs[:6]
+    refs = list(refs[6:])
+
+    def take(count):
+        got = refs[:count]
+        del refs[:count]
+        return got
+
+    rows, wide, lanes = source.shape
+    gx = lax.axis_index("gx")
+    gy = lax.axis_index("gy")
+    (work, hold) = take(2)
+    one = dict(zip(("fx", "lx", "fz", "lz", "rec", "lr", "rat", "first", "last", "f", "u"), take(11)))
+    (edge_fy, edge_ly) = take(2)
+    (sx, rx, sy, ry) = take(4)
+    (coef_s, coef_r, rhs_s, rhs_r) = take(4)
+    (face_s, face_r, back_s, back_r, face2_s, face2_r, back2_s, back2_r) = take(8)
+    (red, terms, whole_prev, whole_next) = take(4)
+    (xu_s, xu_r, xv_s, xv_r, h2_s, h2_r, h3_s, h3_r) = take(8)
+    (c3_s, c3_r, g3_s, g3_r) = take(4)
+    for level in levels:
+        level.bind(take(len(Coarse.names)))
+    (near_send, near_recv, all_send, all_recv, side_send, side_recv) = take(6)
+
+    def far(src, dst, send, recv, device):
+        return pltpu.make_async_remote_copy(
+            src_ref=src, dst_ref=dst, send_sem=send, recv_sem=recv, device_id=device, device_id_type=MESH
+        )
+
+    def beside_copies(src, dst, slot, axis):
+        place, count = (gx, ngx) if axis == 0 else (gy, ngy)
+        higher = (gx + 1, gy) if axis == 0 else (gx, gy + 1)
+        lower = (gx - 1, gy) if axis == 0 else (gx, gy - 1)
+        up = far(src.at[0], dst.at[0], near_send.at[slot, 0], near_recv.at[slot, 0], higher)
+        down = far(src.at[1], dst.at[1], near_send.at[slot, 1], near_recv.at[slot, 1], lower)
+        return place, count, up, down
+
+    def beside_start(src, dst, slot, axis):
+        place, count, up, down = beside_copies(src, dst, slot, axis)
+
+        @pl.when(place < count - 1)
+        def _():
+            up.start()
+
+        @pl.when(place > 0)
+        def _():
+            down.start()
+
+    def beside_wait(src, dst, slot, axis):
+        place, count, up, down = beside_copies(src, dst, slot, axis)
+
+        @pl.when(place < count - 1)
+        def _():
+            up.wait_send()
+            down.wait_recv()
+
+        @pl.when(place > 0)
+        def _():
+            down.wait_send()
+            up.wait_recv()
+
+    def all_start(src, dst, slot):
+        def step(j, carry):
+            peer = lax.rem(gy + j, ngy)
+            far(src(peer), dst.at[gy], all_send.at[slot, peer], all_recv.at[slot, gy], (gx, peer)).start()
+            return carry
+
+        lax.fori_loop(1, ngy, step, 0)
+
+    def all_wait(src, dst, slot):
+        def step(j, carry):
+            peer = lax.rem(gy + j, ngy)
+            far(src(peer), dst.at[peer], all_send.at[slot, peer], all_recv.at[slot, peer], (gx, peer)).wait()
+            return carry
+
+        lax.fori_loop(1, ngy, step, 0)
+
+    def side_start(src, dst, slot):
+        for j in range(1, ngx):
+            peer = lax.rem(gx + j, ngx)
+            far(src, dst.at[gx], side_send.at[slot, j], side_recv.at[slot, gx], (peer, gy)).start()
+
+    def side_wait(src, dst, slot):
+        for j in range(1, ngx):
+            peer = lax.rem(gx + j, ngx)
+            far(src, dst.at[peer], side_send.at[slot, j], side_recv.at[slot, peer], (peer, gy)).wait()
+
+    for ref in (rx, ry, xu_r, xv_r, h2_r, h3_r):
+        ref[...] = jnp.zeros_like(ref)
+    barrier = pltpu.get_barrier_semaphore()
+
+    def greet(j, carry):
+        pl.semaphore_signal(barrier, inc=1, device_id=(gx, lax.rem(gy + j, ngy)), device_id_type=MESH)
+        return carry
+
+    lax.fori_loop(1, ngy, greet, 0)
+    for j in range(1, ngx):
+        pl.semaphore_signal(barrier, inc=1, device_id=(lax.rem(gx + j, ngx), gy), device_id_type=MESH)
+    pl.semaphore_wait(barrier, ngy - 1 + ngx - 1)
+
+    row = lax.broadcasted_iota(jnp.int32, (wide, lanes), 0)
+    lane = lax.broadcasted_iota(jnp.int32, (wide, lanes), 1)
+    opened = [jnp.where(mask[y] != 2, 1.0, 0.0) for y in range(rows)]
+    for y in range(rows):
+        sx[0, pl.ds(y, 1), :] = (cond_x[y] * opened[y])[wide - 1 :]
+        sx[1, pl.ds(y, 1), :] = opened[y][:1]
+    sy[0] = cond_y[rows - 1] * opened[rows - 1]
+    sy[1] = opened[0]
+    beside_start(sx, rx, 0, 0)
+    beside_start(sy, ry, 1, 1)
+    beside_wait(sx, rx, 0, 0)
+    beside_wait(sy, ry, 1, 1)
+    faces_y = []
+    lows_y = [ry[0] * opened[0]]
+    shifts = []
+    for y in range(rows):
+        now = opened[y]
+        cx = cond_x[y] * now
+        one["fx"][y] = cx * jnp.where(row == wide - 1, rx[1, pl.ds(y, 1), :], pltpu.roll(now, wide - 1, 0))
+        one["lx"][y] = now * jnp.where(row == 0, rx[0, pl.ds(y, 1), :], pltpu.roll(cx, 1, 0))
+        above = opened[y + 1] if y + 1 < rows else ry[1]
+        faces_y.append(cond_y[y] * now * above)
+        if y + 1 < rows:
+            lows_y.append(faces_y[y])
+        fz = cond_z[y] * now * jnp.where(lane == lanes - 1, 0.0, pltpu.roll(now, lanes - 1, 1))
+        one["fz"][y] = fz
+        one["lz"][y] = pltpu.roll(fz, 1, 1)
+        shifts.append(base_shift + wall_term * jnp.where(mask[y] == 1, 1.0, 0.0))
+        one["f"][y] = source[y] * now
+    edge_fy[...] = faces_y[rows - 1]
+    edge_ly[...] = lows_y[0]
+
+    half = rows // 2
+    quarter = rows // 4
+    wide2 = wide // 2
+    both = lanes // 2
+
+    def packed(flat):
+        whole = flat.reshape(half, wide2, lanes)
+        return whole[:quarter] + pltpu.roll(whole[quarter:], both, 2)
+
+    coarse_fx = coarsened(one["fx"][...], work, x_odd=True)
+    coef_s[pl.ds(0, quarter)] = packed(coarse_fx)
+    coef_s[pl.ds(quarter, quarter)] = packed(coarsened(jnp.stack(faces_y), work, y_odd=True))
+    coef_s[pl.ds(2 * quarter, quarter)] = packed(coarsened(one["fz"][...], work, z_odd=True))
+    coef_s[pl.ds(3 * quarter, quarter)] = packed(coarsened(jnp.stack(shifts), work))
+    lx_all = one["lx"][...].reshape(half, 2, wide, lanes)
+    lx_rows = (lx_all[:, 0] + lx_all[:, 1]).reshape(half * wide, lanes)
+    work[pl.ds(0, half * wide), :] = times(lx_rows, pairing(None))
+    for y in range(half):
+        coef_s[4 * quarter, pl.ds(y, 1), :] = 0.25 * work[pl.ds(y * wide, 1), :]
+    coef_r[gy] = coef_s[...]
+    all_start(lambda peer: coef_s, coef_r, 0)
+
+    recs = []
+    ratio = None
+    for y in range(rows):
+        diag = shifts[y] + one["fx"][y] + one["lx"][y] + faces_y[y] + lows_y[y] + one["fz"][y] + one["lz"][y]
+        if y:
+            diag = diag - lows_y[y] * ratio
+        rec = 1.0 / diag
+        ratio = faces_y[y] * rec
+        recs.append(rec)
+        one["rec"][y] = rec
+        one["rat"][y] = ratio
+        one["lr"][y] = lows_y[y] * rec
+
+    def block_solve(right):
+        value = right[0] * one["rec"][0]
+        values = [value]
+        for y in range(1, rows):
+            value = right[y] * one["rec"][y] + one["lr"][y] * value
+            values.append(value)
+        for y in range(rows - 2, -1, -1):
+            values[y] = values[y] + one["rat"][y] * values[y + 1]
+        return values
+
+    firsts = [recs[0]]
+    for y in range(1, rows):
+        firsts.append(one["lr"][y] * firsts[-1])
+    lasts = [None] * (rows - 1) + [recs[rows - 1]]
+    for y in range(rows - 2, -1, -1):
+        firsts[y] = firsts[y] + one["rat"][y] * firsts[y + 1]
+        lasts[y] = one["rat"][y] * lasts[y + 1]
+    low, high = edge_ly[...], edge_fy[...]
+    for y in range(rows):
+        firsts[y] = low * firsts[y]
+        lasts[y] = high * lasts[y]
+        one["first"][y] = firsts[y]
+        one["last"][y] = lasts[y]
+    share = wide // ngy
+
+    def shared(target, values):
+        for place, value in enumerate(values):
+            for owner in range(ngy):
+                target[owner, place] = value[owner * share : (owner + 1) * share]
+
+    def reduced(rhs, send):
+        zero = jnp.zeros((share, lanes), jnp.float32)
+
+        def down(k, carry):
+            p = carry
+            start = (rhs[k, 0] + face_r[k, 0] * p) * red[k, 1]
+            terms[k, 0] = start
+            terms[k, 1] = p
+            return rhs[k, 1] + face_r[k, 2] * (p + red[k, 0] * start)
+
+        def up(step, after):
+            k = ngy - 1 - step
+            first = terms[k, 0] + red[k, 2] * after
+            send[k, 0] = terms[k, 1] + red[k, 0] * first
+            send[k, 1] = after
+            return first
+
+        looped(ngy, down, zero)
+        looped(ngy, up, zero)
+
+    def reduced_factor():
+        def step(k, q):
+            inv = 1.0 / (1.0 - face_r[k, 0] * q)
+            slope = face_r[k, 1] * inv
+            red[k, 0] = q
+            red[k, 1] = inv
+            red[k, 2] = slope
+            return face_r[k, 3] + face_r[k, 2] * q * slope
+
+        looped(ngy, step, jnp.zeros((share, lanes), jnp.float32))
+
+    def joined(local, got):
+        for owner in range(ngy):
+            whole_prev[pl.ds(owner * share, share), :] = got[owner, 0]
+            whole_next[pl.ds(owner * share, share), :] = got[owner, 1]
+        prev, after = whole_prev[...], whole_next[...]
+        return [local[y] + prev * one["first"][y] + after * one["last"][y] for y in range(rows)]
+
+    local = block_solve([one["f"][y] for y in range(rows)])
+    shared(face_s, [firsts[0], lasts[0], firsts[rows - 1], lasts[rows - 1], local[0], local[rows - 1]])
+    face_r[gy] = face_s[gy]
+    all_start(lambda peer: face_s.at[peer], face_r, 1)
+    all_wait(lambda peer: face_s.at[peer], face_r, 1)
+    reduced_factor()
+    reduced(face_r.at[:, pl.ds(4, 2)], back_s)
+    back_r[gy] = back_s[gy]
+    all_start(lambda peer: back_s.at[peer], back_r, 2)
+    all_wait(lambda peer: back_s.at[peer], back_r, 2)
+    values = joined(local, back_r)
+
+    def outer_planes(values, target):
+        for y in range(rows):
+            target[0, pl.ds(y, 1), :] = values[y][wide - 1 :]
+            target[1, pl.ds(y, 1), :] = values[y][:1]
+
+    def beside_one(y, u, got):
+        return (
+            one["fx"][y] * jnp.where(row == wide - 1, got[1, pl.ds(y, 1), :], pltpu.roll(u, wide - 1, 0))
+            + one["lx"][y] * jnp.where(row == 0, got[0, pl.ds(y, 1), :], pltpu.roll(u, 1, 0))
+            + one["fz"][y] * pltpu.roll(u, lanes - 1, 1)
+            + one["lz"][y] * pltpu.roll(u, 1, 1)
+        )
+
+    outer_planes(values, xu_s)
+    beside_start(xu_s, xu_r, 2, 0)
+    for y in range(rows):
+        one["u"][y] = values[y]
+    beside_wait(xu_s, xu_r, 2, 0)
+    left = jnp.stack([beside_one(y, values[y], xu_r) for y in range(rows)])
+    rhs_s[...] = packed(coarsened(left, work))
+    rhs_r[gy] = rhs_s[...]
+    all_start(lambda peer: rhs_s, rhs_r, 3)
+
+    two, three = levels[0], levels[1]
+    used = lax.broadcasted_iota(jnp.int32, (wide2, lanes), 1) < both
+
+    def unpack2(target, block, k):
+        for y in range(quarter):
+            pair = block(y)
+            target[half * k + y] = jnp.where(used, pair, 0.0)
+            target[half * k + quarter + y] = jnp.where(used, pltpu.roll(pair, both, 1), 0.0)
+
+    all_wait(lambda peer: coef_s, coef_r, 0)
+
+    def take_coefs(k, carry):
+        for place, target in enumerate((two.fx, two.fy, two.fz, two.sh)):
+            unpack2(target, lambda y: coef_r[k, place * quarter + y], k)
+        return carry
+
+    lax.fori_loop(0, ngy, take_coefs, 0)
+
+    rows3 = three.rows
+    part3 = rows3 // 4
+    wide3 = wide2 // 2
+    step3 = lanes // 4
+
+    def packed3(flat):
+        whole = flat.reshape(rows3, wide3, lanes)
+        total = whole[:part3]
+        for j in range(1, 4):
+            total = total + pltpu.roll(whole[j * part3 : (j + 1) * part3], j * step3, 2)
+        return total
+
+    used3 = lax.broadcasted_iota(jnp.int32, (part3, wide3, lanes), 2) < step3
+
+    def unpack3(target, got):
+        for g in range(ngx):
+            block = got(g)
+            for j in range(4):
+                turned = block if j == 0 else pltpu.roll(block, lanes - j * step3, 2)
+                target[pl.ds(j * part3, part3), pl.ds(g * wide3, wide3), :] = jnp.where(used3, turned, 0.0)
+
+    c3_s[0] = packed3(coarsened(two.fx[...], work, x_odd=True))
+    c3_s[1] = packed3(coarsened(two.fy[...], work, y_odd=True))
+    c3_s[2] = packed3(coarsened(two.fz[...], work, z_odd=True))
+    c3_s[3] = packed3(coarsened(two.sh[...], work))
+    c3_r[gx] = c3_s[...]
+    side_start(c3_s, c3_r, 0)
+
+    def edge2(y):
+        return h2_s[0, pl.ds(y, 1), :]
+
+    def take_edges(k, carry):
+        for y in range(half):
+            h2_s[0, pl.ds(half * k + y, 1), :] = coef_r[k, 4 * quarter, pl.ds(y, 1), :]
+        return carry
+
+    lax.fori_loop(0, ngy, take_edges, 0)
+    two.factor(edge2)
+    all_wait(lambda peer: rhs_s, rhs_r, 3)
+
+    def take_rhs(k, carry):
+        unpack2(two.g, lambda y: rhs_r[k, y], k)
+        return carry
+
+    lax.fori_loop(0, ngy, take_rhs, 0)
+    two.solve(False)
+
+    def outer_two(target):
+        def step(y, carry):
+            target[0, pl.ds(y, 1), :] = two.u[y, pl.ds(wide2 - 1, 1), :]
+            target[1, pl.ds(y, 1), :] = two.u[y, pl.ds(0, 1), :]
+            return carry
+
+        looped(two.rows, step, 0)
+
+    outer_two(h2_s)
+    beside_start(h2_s, h2_r, 3, 0)
+    side_wait(c3_s, c3_r, 0)
+    for place, target in enumerate((three.fx, three.fy, three.fz, three.sh)):
+        unpack3(target, lambda g: c3_r[g, place])
+    for fine, level in zip(levels[1:], levels[2:]):
+        put_rows(level.fx, coarsened(fine.fx[...], work, x_odd=True), level.rows)
+        put_rows(level.fy, coarsened(fine.fy[...], work, y_odd=True), level.rows)
+        put_rows(level.fz, coarsened(fine.fz[...], work, z_odd=True), level.rows)
+        put_rows(level.sh, coarsened(fine.sh[...], work), level.rows)
+    for level in levels[1:]:
+        level.factor()
+    beside_wait(h2_s, h2_r, 3, 0)
+    two.halo = h2_r
+    two.residual(hold)
+    g3_s[...] = packed3(coarsened(hold[...], work))
+    g3_r[gx] = g3_s[...]
+    side_start(g3_s, g3_r, 1)
+    side_wait(g3_s, g3_r, 1)
+    unpack3(three.g, lambda g: g3_r[g])
+    for fine, level in zip(levels[1:], levels[2:]):
+        fine.solve(False)
+        part = hold.at[pl.ds(0, fine.rows), pl.ds(0, fine.wide)]
+        fine.residual(part)
+        put_rows(level.g, coarsened(part[...], work), level.rows)
+    levels[-1].solve(False)
+    levels[-1].solve(True)
+    for fine, level in zip(levels[-2:0:-1], levels[:1:-1]):
+        spread_add(fine.u, level.u[...], fine.wide, work)
+        fine.solve(True)
+    spread_add(two.u, three.u[:, pl.ds(pl.multiple_of(gx * wide3, 8), wide3), :], wide2, work)
+    outer_two(h3_s)
+    beside_start(h3_s, h3_r, 4, 0)
+    beside_wait(h3_s, h3_r, 4, 0)
+    two.halo = h3_r
+    two.solve(True)
+    spread_add(one["u"], two.u[pl.ds(gy * half, half)], wide, work)
+    values = [one["u"][y] for y in range(rows)]
+    outer_planes(values, xv_s)
+    beside_start(xv_s, xv_r, 5, 0)
+    beside_wait(xv_s, xv_r, 5, 0)
+    local = block_solve([one["f"][y] + beside_one(y, values[y], xv_r) for y in range(rows)])
+    shared(face2_s, [local[0], local[rows - 1]])
+    face2_r[gy] = face2_s[gy]
+    all_start(lambda peer: face2_s.at[peer], face2_r, 4)
+    all_wait(lambda peer: face2_s.at[peer], face2_r, 4)
+    reduced(face2_r, back2_s)
+    back2_r[gy] = back2_s[gy]
+    all_start(lambda peer: back2_s.at[peer], back2_r, 5)
+    all_wait(lambda peer: back2_s.at[peer], back2_r, 5)
+    values = joined(local, back2_r)
+    for y in range(rows):
+        out[y] = values[y]
+
+
+def fused(ngx, ngy, *args):
+    rows, wide, lanes = args[0].shape
+    f32 = jnp.float32
+    levels = [Coarse(rows // 2 * ngy, wide // 2, lanes // 2)]
+    for depth in range(2, LEVELS):
+        whole = wide * ngx >> depth
+        levels.append(Coarse(rows * ngy >> depth, whole, lanes >> depth))
+    two, three = levels[:2]
+    share = wide // ngy
+    quarter = rows // 4
+    wide2 = wide // 2
+
+    def room(*shape):
+        return pltpu.VMEM(shape, f32)
+
+    part3 = three.rows // 4
+    wide3 = wide2 // 2
+    most = max(rows * wide, two.rows * two.wide, three.rows * three.wide)
+    scratch = [room(most, lanes), room(two.rows, two.wide, lanes)]
+    scratch += [room(rows, wide, lanes)] * 11
+    scratch += [room(wide, lanes)] * 2
+    scratch += [room(2, rows, lanes)] * 2 + [room(2, wide, lanes)] * 2
+    count = 4 * quarter + 1
+    scratch += [room(count, wide2, lanes), room(ngy, count, wide2, lanes)]
+    scratch += [room(quarter, wide2, lanes), room(ngy, quarter, wide2, lanes)]
+    scratch += [room(ngy, 6, share, lanes)] * 2 + [room(ngy, 2, share, lanes)] * 6
+    scratch += [room(ngy, 3, share, lanes), room(ngy, 2, share, lanes)]
+    scratch += [room(wide, lanes)] * 2
+    scratch += [room(2, rows, lanes)] * 4 + [room(2, two.rows, lanes)] * 4
+    scratch += [room(4, part3, wide3, lanes), room(ngx, 4, part3, wide3, lanes)]
+    scratch += [room(part3, wide3, lanes), room(ngx, part3, wide3, lanes)]
+    for level in levels:
+        scratch += level.scratch()
+    dma = pltpu.SemaphoreType.DMA
+    scratch += [dma((6, 2)), dma((6, 2)), dma((6, ngy)), dma((6, ngy)), dma((2, ngx)), dma((2, ngx))]
+    return pl.pallas_call(
+        functools.partial(v_cycle_kernel, ngx, ngy, levels),
+        out_shape=jax.ShapeDtypeStruct(args[0].shape, f32),
+        in_specs=[pl.BlockSpec(memory_space=pltpu.VMEM)] * 5,
+        out_specs=pl.BlockSpec(memory_space=pltpu.VMEM),
+        scratch_shapes=scratch,
+        compiler_params=pltpu.CompilerParams(
+            collective_id=0, has_side_effects=True, vmem_limit_bytes=48 * 2**20
+        ),
+    )(*args)
+
 
 def solution(mesh):
+    ngx, ngy = mesh.shape["gx"], mesh.shape["gy"]
+    small = ngy <= 16 and ngx <= 4
+    part = functools.partial(fused, ngx, ngy) if small else body
     return jax.shard_map(
-        body,
+        part,
         mesh=mesh,
-        in_specs=(
-            P("gy", "gx", None),
-            P("gy", "gx", None),
-            P("gy", "gx", None),
-            P("gy", "gx", None),
-            P("gy", "gx", None),
-        ),
+        in_specs=(P("gy", "gx", None),) * 5,
         out_specs=P("gy", "gx", None),
         check_vma=False,
     )

time: 844 us -> 89.2 us (0.11); the launches traced: 829 us -> 89 us
  local copies, waits for them, and re-layouts: 389 us -> 5.18 us
  blocking collectives: 165 us -> 0 us
  starting transfers between devices: 104 us -> 0 us
  other arithmetic: 103 us -> 0 us
  Pallas kernels: 0 us -> 83.9 us
  waiting for transfers between devices: 61.6 us -> 0 us
    slice x634 -> x0, local copies, waits for them, and re-layouts: 293 us -> none  [the longest x4 174 us: reduced_moved(): moved[1]]
    all_gather x8 -> x0, blocking collectives: 146 us -> none  [reduced_moved(): whole = lax.all_gather(packed, 'gy', axis=1, tiled=True)]
    pallas_call x0 -> x1, Pallas kernels: none -> 83.9 us  [fused(): pl.pallas_call(functools.partial(v_cycle_kernel, ngx, ngy, levels), out_s...]
    ppermute x30 -> x0, starting transfers between devices: 75 us -> none  [the longest x13 56.4 us: padded(): lax.ppermute(tail, axis, [(i, (i + 1) % count) for i in range(ends)])]
    unnamed x37 -> x0, other arithmetic: 47.2 us -> none
    reshape x25 -> x0, local copies, waits for them, and re-layouts: 33.8 us -> none  [the longest x5 32 us: coarse_sum(): field.reshape(depth // 2, 2, width // 2, 2, height // 2, 2)]
    all_to_all x6 -> x0, waiting for transfers between devices: 31.6 us -> none  [the longest x3 18.2 us: reduced_moved(): lax.all_to_all(jnp.stack([prev_last, next_first]), 'gy', split_axis=1, co...]
    ppermute x30 -> x0, waiting for transfers between devices: 29.9 us -> none  [the longest x4 11.7 us: swapped(): lax.ppermute(x, axis, [(i, i ^ 1 << stride) for i in range(lax.axis_size(...]
  transfers between devices with their start and end apart: 36 -> 0, of which waited for: 22 -> 0; matrix products, arithmetic and copies ran while one was open for 5% -> 0% of each run, Pallas kernels for 0% -> 0%
where the time goes in v1:
time: 89.2 us; the launch traced here: 89 us
  Pallas kernels  83.9 us (94%)
  local copies, waits for them, and re-layouts  5.18 us (6%)
    pallas_call x1, Pallas kernels, fused(): pl.pallas_call(functools.partial(v_cycle_kernel, ngx, ngy, levels), out_s...  83.9 us
    unnamed x11, local copies, waits for them, and re-layouts  5.18 us

profile of v1, /device:TPU:0, one launch (start us, length us, event | category | flops | bytes accessed | tf_op | source)
XLA Modules:
  0.0 89.0 jit_solution(17958531555564207491)
XLA Ops:
  0.0 0.0 copy-start
  0.0 0.9 %copy-done = f32[8,32,128]{2,1,0:T(8,128)S(1)} copy-done((f32[8,32,128]{2,1,0:T(8,128)S(1)}, f32[8,32,128]{2,1,0:T(8,128)}, u32[]{:S(2)}) %copy-start) | copy-done | bytes 131096
  0.9 0.0 copy-start.1
  0.9 0.9 %copy-done.1 = s32[8,32,128]{2,1,0:T(8,128)S(1)} copy-done((s32[8,32,128]{2,1,0:T(8,128)S(1)}, s32[8,32,128]{2,1,0:T(8,128)}, u32[]{:S(2)}) %copy-start.1) | copy-done | bytes 131096
  1.8 0.0 copy-start.2
  1.8 0.9 %copy-done.2 = f32[8,32,128]{2,1,0:T(8,128)S(1)} copy-done((f32[8,32,128]{2,1,0:T(8,128)S(1)}, f32[8,32,128]{2,1,0:T(8,128)}, u32[]{:S(2)}) %copy-start.2) | copy-done | bytes 131096
  2.7 0.0 copy-start.3
  2.7 0.9 %copy-done.3 = f32[8,32,128]{2,1,0:T(8,128)S(1)} copy-done((f32[8,32,128]{2,1,0:T(8,128)S(1)}, f32[8,32,128]{2,1,0:T(8,128)}, u32[]{:S(2)}) %copy-start.3) | copy-done | bytes 131096
  3.6 0.0 copy-start.4
  3.6 0.9 %copy-done.4 = f32[8,32,128]{2,1,0:T(8,128)S(1)} copy-done((f32[8,32,128]{2,1,0:T(8,128)S(1)}, f32[8,32,128]{2,1,0:T(8,128)}, u32[]{:S(2)}) %copy-start.4) | copy-done | bytes 131096
  4.5 83.9 %shard_map.55 = f32[8,32,128]{2,1,0:T(8,128)S(1)} custom-call(f32[8,32,128]{2,1,0:T(8,128)S(1)} %copy-done, s32[8,32,128]{2,1,0:T(8,128)S(1)} %copy-done.1, f32[8,32,128]{2,1,0:T(8,128)S(1)} %copy-done.2, f32[8,32,128]{2,1,0:T(8,128)S(1)} %copy-done.3, f32[8,32,128]{2,1,0:T(8,128)S(1)} %copy-done.4), custom_call_target="tpu_custom_call" | custom-call | tf_op jit(solution)/shard_map/pallas_call | solution.py:879
  88.4 0.7 copy.7
Async XLA Ops:
  0.0 0.9 %copy-start = (f32[8,32,128]{2,1,0:T(8,128)S(1)}, f32[8,32,128]{2,1,0:T(8,128)}, u32[]{:S(2)}) copy-start(f32[8,32,128]{2,1,0:T(8,128)} %refs_0_.1) | copy-start | bytes 393220
  0.9 0.9 %copy-start.1 = (s32[8,32,128]{2,1,0:T(8,128)S(1)}, s32[8,32,128]{2,1,0:T(8,128)}, u32[]{:S(2)}) copy-start(s32[8,32,128]{2,1,0:T(8,128)} %refs_1_.1) | copy-start | bytes 393220
  1.8 0.9 %copy-start.2 = (f32[8,32,128]{2,1,0:T(8,128)S(1)}, f32[8,32,128]{2,1,0:T(8,128)}, u32[]{:S(2)}) copy-start(f32[8,32,128]{2,1,0:T(8,128)} %refs_2_.1) | copy-start | bytes 393220
  2.7 0.9 %copy-start.3 = (f32[8,32,128]{2,1,0:T(8,128)S(1)}, f32[8,32,128]{2,1,0:T(8,128)}, u32[]{:S(2)}) copy-start(f32[8,32,128]{2,1,0:T(8,128)} %refs_3_.1) | copy-start | bytes 393220
  3.6 0.9 %copy-start.4 = (f32[8,32,128]{2,1,0:T(8,128)S(1)}, f32[8,32,128]{2,1,0:T(8,128)}, u32[]{:S(2)}) copy-start(f32[8,32,128]{2,1,0:T(8,128)} %refs_4_.1) | copy-start | bytes 393220

commit v2 on v1

--- a/solution.py
+++ b/solution.py
@@ -287,7 +287,6 @@
 
 MESH = pl.DeviceIdType.MESH
 LANES = 128
-EXACT = lax.Precision.HIGHEST
 
 
 def looped(count, step, carry, unroll=4):
@@ -320,14 +319,23 @@
 
 
 def times(left, right):
-    return jnp.dot(left, right, precision=EXACT, preferred_element_type=jnp.float32)
-
-
-def coarsened(field, work, y_odd=False, x_odd=False, z_odd=False):
-    rows, wide, lanes = field.shape
-    pairs = field.reshape(rows // 2, 2, wide, lanes)
-    summed = pairs[:, 1] if y_odd else pairs[:, 0] + pairs[:, 1]
-    count = rows // 2 * wide
+    right = right.astype(jnp.bfloat16)
+    head = left.astype(jnp.bfloat16)
+    tail = (left - head.astype(jnp.float32)).astype(jnp.bfloat16)
+    return jnp.dot(head, right, preferred_element_type=jnp.float32) + jnp.dot(
+        tail, right, preferred_element_type=jnp.float32
+    )
+
+
+def coarsened(field, work, y_odd=False, x_odd=False, z_odd=False, y_summed=False):
+    if y_summed:
+        summed = field
+    else:
+        rows, wide, lanes = field.shape
+        pairs = field.reshape(rows // 2, 2, wide, lanes)
+        summed = pairs[:, 1] if y_odd else pairs[:, 0] + pairs[:, 1]
+    rows, wide, lanes = summed.shape
+    count = rows * wide
     work[pl.ds(0, count), :] = times(summed.reshape(count, lanes), pairing(1 if z_odd else None))
     result = work[pl.ds(1, count // 2, stride=2), :]
     if not x_odd:
@@ -436,14 +444,14 @@
 
     def residual(self, hold):
         def step(y, carry):
-            hold[y] = self.beside(y)
+            hold[y] = self.beside(2 * y) + self.beside(2 * y + 1)
             return carry
 
-        looped(self.rows, step, 0)
+        looped(self.rows // 2, step, 0)
 
 
 def v_cycle_kernel(ngx, ngy, levels, *refs):
-    source, mask, cond_x, cond_y, cond_z, out = refs[:6]
+    given, out = refs[:5], refs[5]
     refs = list(refs[6:])
 
     def take(count):
@@ -451,9 +459,11 @@
         del refs[:count]
         return got
 
-    rows, wide, lanes = source.shape
+    rows, wide, lanes = given[0].shape
     gx = lax.axis_index("gx")
     gy = lax.axis_index("gy")
+    inside = take(5)
+    (source, mask, cond_x, cond_y, cond_z) = inside
     (work, hold) = take(2)
     one = dict(zip(("fx", "lx", "fz", "lz", "rec", "lr", "rat", "first", "last", "f", "u"), take(11)))
     (edge_fy, edge_ly) = take(2)
@@ -461,11 +471,16 @@
     (coef_s, coef_r, rhs_s, rhs_r) = take(4)
     (face_s, face_r, back_s, back_r, face2_s, face2_r, back2_s, back2_r) = take(8)
     (red, terms, whole_prev, whole_next) = take(4)
-    (xu_s, xu_r, xv_s, xv_r, h2_s, h2_r, h3_s, h3_r) = take(8)
+    (xu_s, xu_r, xv_s, xv_r, h2_s, h2_r) = take(6)
     (c3_s, c3_r, g3_s, g3_r) = take(4)
     for level in levels:
         level.bind(take(len(Coarse.names)))
-    (near_send, near_recv, all_send, all_recv, side_send, side_recv) = take(6)
+    (near_send, near_recv, all_send, all_recv, side_send, side_recv, load_sem) = take(7)
+    loads = [pltpu.make_async_copy(a, b, load_sem.at[i]) for i, (a, b) in enumerate(zip(given, inside))]
+    for load in loads:
+        load.start()
+    (tree_send, tree_recv) = take(2)
+    peers = [lax.rem(gy + j, ngy) for j in range(1, ngy)]
 
     def far(src, dst, send, recv, device):
         return pltpu.make_async_remote_copy(
@@ -505,20 +520,60 @@
             up.wait_recv()
 
     def all_start(src, dst, slot):
-        def step(j, carry):
-            peer = lax.rem(gy + j, ngy)
-            far(src(peer), dst.at[gy], all_send.at[slot, peer], all_recv.at[slot, gy], (gx, peer)).start()
-            return carry
-
-        lax.fori_loop(1, ngy, step, 0)
-
-    def all_wait(src, dst, slot):
-        def step(j, carry):
-            peer = lax.rem(gy + j, ngy)
-            far(src(peer), dst.at[peer], all_send.at[slot, peer], all_recv.at[slot, peer], (gx, peer)).wait()
-            return carry
-
-        lax.fori_loop(1, ngy, step, 0)
+        for peer in peers:
+            far(src(peer), dst.at[gy], all_send.at[slot], all_recv.at[slot], (gx, peer)).start()
+
+    def all_wait(dst, slot):
+        others = dst.at[pl.ds(0, ngy - 1)]
+        far(others, others, all_send.at[slot], all_recv.at[slot], (gx, peers[0])).wait()
+
+    far_count = ngy // 4
+    place_a = gy // 4
+    place_b = lax.rem(gy // 2, 2)
+    place_c = lax.rem(gy, 2)
+
+    def tree_slot(k):
+        return (lax.rem(k, 2) * 2 + lax.rem(k // 2, 2)) * far_count + k // 4
+
+    def tree_copies(stage):
+        if stage == 0:
+            copies = []
+            for j in range(1, far_count):
+                a = lax.rem(place_a + j, far_count)
+                slot = tree_slot(gy)
+                peer = a * 4 + place_b * 2 + place_c
+                there = far_count - j
+                copies.append(
+                    (
+                        far(coef_s, coef_r.at[slot], tree_send.at[j], tree_recv.at[j], (gx, peer)),
+                        far(coef_s, coef_r.at[tree_slot(peer)], tree_send.at[j], tree_recv.at[there], (gx, peer)),
+                    )
+                )
+            return copies
+        if stage == 1:
+            mine = coef_r.at[pl.ds((place_c * 2 + place_b) * far_count, far_count)]
+            theirs = coef_r.at[pl.ds((place_c * 2 + 1 - place_b) * far_count, far_count)]
+            peer = place_a * 4 + (1 - place_b) * 2 + place_c
+        else:
+            mine = coef_r.at[pl.ds(place_c * 2 * far_count, 2 * far_count)]
+            theirs = coef_r.at[pl.ds((1 - place_c) * 2 * far_count, 2 * far_count)]
+            peer = place_a * 4 + place_b * 2 + 1 - place_c
+        slot = ngy + stage - 1
+        return [
+            (
+                far(mine, mine, tree_send.at[slot], tree_recv.at[slot], (gx, peer)),
+                far(mine, theirs, tree_send.at[slot], tree_recv.at[slot], (gx, peer)),
+            )
+        ]
+
+    def tree_start(stage):
+        for outgoing, incoming in tree_copies(stage):
+            outgoing.start()
+
+    def tree_wait(stage):
+        for outgoing, incoming in tree_copies(stage):
+            outgoing.wait_send()
+            incoming.wait_recv()
 
     def side_start(src, dst, slot):
         for j in range(1, ngx):
@@ -530,17 +585,16 @@
             peer = lax.rem(gx + j, ngx)
             far(src, dst.at[peer], side_send.at[slot, j], side_recv.at[slot, peer], (peer, gy)).wait()
 
-    for ref in (rx, ry, xu_r, xv_r, h2_r, h3_r):
+    for ref in (rx, ry, xu_r, xv_r, h2_r):
         ref[...] = jnp.zeros_like(ref)
     barrier = pltpu.get_barrier_semaphore()
 
-    def greet(j, carry):
-        pl.semaphore_signal(barrier, inc=1, device_id=(gx, lax.rem(gy + j, ngy)), device_id_type=MESH)
-        return carry
-
-    lax.fori_loop(1, ngy, greet, 0)
+    for peer in peers:
+        pl.semaphore_signal(barrier, inc=1, device_id=(gx, peer), device_id_type=MESH)
     for j in range(1, ngx):
         pl.semaphore_signal(barrier, inc=1, device_id=(lax.rem(gx + j, ngx), gy), device_id_type=MESH)
+    for load in loads:
+        load.wait()
     pl.semaphore_wait(barrier, ngy - 1 + ngx - 1)
 
     row = lax.broadcasted_iota(jnp.int32, (wide, lanes), 0)
@@ -575,28 +629,6 @@
     edge_fy[...] = faces_y[rows - 1]
     edge_ly[...] = lows_y[0]
 
-    half = rows // 2
-    quarter = rows // 4
-    wide2 = wide // 2
-    both = lanes // 2
-
-    def packed(flat):
-        whole = flat.reshape(half, wide2, lanes)
-        return whole[:quarter] + pltpu.roll(whole[quarter:], both, 2)
-
-    coarse_fx = coarsened(one["fx"][...], work, x_odd=True)
-    coef_s[pl.ds(0, quarter)] = packed(coarse_fx)
-    coef_s[pl.ds(quarter, quarter)] = packed(coarsened(jnp.stack(faces_y), work, y_odd=True))
-    coef_s[pl.ds(2 * quarter, quarter)] = packed(coarsened(one["fz"][...], work, z_odd=True))
-    coef_s[pl.ds(3 * quarter, quarter)] = packed(coarsened(jnp.stack(shifts), work))
-    lx_all = one["lx"][...].reshape(half, 2, wide, lanes)
-    lx_rows = (lx_all[:, 0] + lx_all[:, 1]).reshape(half * wide, lanes)
-    work[pl.ds(0, half * wide), :] = times(lx_rows, pairing(None))
-    for y in range(half):
-        coef_s[4 * quarter, pl.ds(y, 1), :] = 0.25 * work[pl.ds(y * wide, 1), :]
-    coef_r[gy] = coef_s[...]
-    all_start(lambda peer: coef_s, coef_r, 0)
-
     recs = []
     ratio = None
     for y in range(rows):
@@ -682,12 +714,36 @@
     shared(face_s, [firsts[0], lasts[0], firsts[rows - 1], lasts[rows - 1], local[0], local[rows - 1]])
     face_r[gy] = face_s[gy]
     all_start(lambda peer: face_s.at[peer], face_r, 1)
-    all_wait(lambda peer: face_s.at[peer], face_r, 1)
+
+    half = rows // 2
+    quarter = rows // 4
+    wide2 = wide // 2
+    both = lanes // 2
+
+    def packed(flat):
+        whole = flat.reshape(half, wide2, lanes)
+        return whole[:quarter] + pltpu.roll(whole[quarter:], both, 2)
+
+    coarse_fx = coarsened(one["fx"][...], work, x_odd=True)
+    coef_s[pl.ds(0, quarter)] = packed(coarse_fx)
+    coef_s[pl.ds(quarter, quarter)] = packed(coarsened(jnp.stack(faces_y), work, y_odd=True))
+    coef_s[pl.ds(2 * quarter, quarter)] = packed(coarsened(one["fz"][...], work, z_odd=True))
+    coef_s[pl.ds(3 * quarter, quarter)] = packed(coarsened(jnp.stack(shifts), work))
+    lx_all = one["lx"][...].reshape(half, 2, wide, lanes)
+    lx_rows = (lx_all[:, 0] + lx_all[:, 1]).reshape(half * wide, lanes)
+    work[pl.ds(0, half * wide), :] = times(lx_rows, pairing(None))
+    for y in range(half):
+        coef_s[4 * quarter, pl.ds(y, 1), :] = 0.25 * work[pl.ds(y * wide, 1), :]
+    coef_r[tree_slot(gy)] = coef_s[...]
+    tree_start(0)
+    all_wait(face_r, 1)
     reduced_factor()
     reduced(face_r.at[:, pl.ds(4, 2)], back_s)
     back_r[gy] = back_s[gy]
     all_start(lambda peer: back_s.at[peer], back_r, 2)
-    all_wait(lambda peer: back_s.at[peer], back_r, 2)
+    tree_wait(0)
+    tree_start(1)
+    all_wait(back_r, 2)
     values = joined(local, back_r)
 
     def outer_planes(values, target):
@@ -707,6 +763,8 @@
     beside_start(xu_s, xu_r, 2, 0)
     for y in range(rows):
         one["u"][y] = values[y]
+    tree_wait(1)
+    tree_start(2)
     beside_wait(xu_s, xu_r, 2, 0)
     left = jnp.stack([beside_one(y, values[y], xu_r) for y in range(rows)])
     rhs_s[...] = packed(coarsened(left, work))
@@ -722,11 +780,11 @@
             target[half * k + y] = jnp.where(used, pair, 0.0)
             target[half * k + quarter + y] = jnp.where(used, pltpu.roll(pair, both, 1), 0.0)
 
-    all_wait(lambda peer: coef_s, coef_r, 0)
+    tree_wait(2)
 
     def take_coefs(k, carry):
         for place, target in enumerate((two.fx, two.fy, two.fz, two.sh)):
-            unpack2(target, lambda y: coef_r[k, place * quarter + y], k)
+            unpack2(target, lambda y: coef_r[tree_slot(k), place * quarter + y], k)
         return carry
 
     lax.fori_loop(0, ngy, take_coefs, 0)
@@ -764,12 +822,12 @@
 
     def take_edges(k, carry):
         for y in range(half):
-            h2_s[0, pl.ds(half * k + y, 1), :] = coef_r[k, 4 * quarter, pl.ds(y, 1), :]
+            h2_s[0, pl.ds(half * k + y, 1), :] = coef_r[tree_slot(k), 4 * quarter, pl.ds(y, 1), :]
         return carry
 
     lax.fori_loop(0, ngy, take_edges, 0)
     two.factor(edge2)
-    all_wait(lambda peer: rhs_s, rhs_r, 3)
+    all_wait(rhs_r, 3)
 
     def take_rhs(k, carry):
         unpack2(two.g, lambda y: rhs_r[k, y], k)
@@ -801,26 +859,33 @@
     beside_wait(h2_s, h2_r, 3, 0)
     two.halo = h2_r
     two.residual(hold)
-    g3_s[...] = packed3(coarsened(hold[...], work))
+    g3_s[...] = packed3(coarsened(hold[...], work, y_summed=True))
     g3_r[gx] = g3_s[...]
     side_start(g3_s, g3_r, 1)
     side_wait(g3_s, g3_r, 1)
     unpack3(three.g, lambda g: g3_r[g])
     for fine, level in zip(levels[1:], levels[2:]):
         fine.solve(False)
-        part = hold.at[pl.ds(0, fine.rows), pl.ds(0, fine.wide)]
+        part = hold.at[pl.ds(0, fine.rows // 2), pl.ds(0, fine.wide)]
         fine.residual(part)
-        put_rows(level.g, coarsened(part[...], work), level.rows)
+        put_rows(level.g, coarsened(part[...], work, y_summed=True), level.rows)
     levels[-1].solve(False)
     levels[-1].solve(True)
     for fine, level in zip(levels[-2:0:-1], levels[:1:-1]):
         spread_add(fine.u, level.u[...], fine.wide, work)
         fine.solve(True)
     spread_add(two.u, three.u[:, pl.ds(pl.multiple_of(gx * wide3, 8), wide3), :], wide2, work)
-    outer_two(h3_s)
-    beside_start(h3_s, h3_r, 4, 0)
-    beside_wait(h3_s, h3_r, 4, 0)
-    two.halo = h3_r
+    for side, plane in enumerate((lax.max(gx * wide3 - 1, 0), lax.min((gx + 1) * wide3, three.width - 1))):
+
+        def pick(y, carry):
+            work[pl.ds(y, 1), :] = three.u[y, pl.ds(plane, 1), :]
+            return carry
+
+        looped(rows3, pick, 0)
+        extra = times(work[pl.ds(0, rows3), :], spreading())
+        work[pl.ds(0, rows3, stride=2), :] = extra
+        work[pl.ds(1, rows3, stride=2), :] = extra
+        h2_r[side] = h2_r[side] + work[pl.ds(0, 2 * rows3), :]
     two.solve(True)
     spread_add(one["u"], two.u[pl.ds(gy * half, half)], wide, work)
     values = [one["u"][y] for y in range(rows)]
@@ -831,11 +896,11 @@
     shared(face2_s, [local[0], local[rows - 1]])
     face2_r[gy] = face2_s[gy]
     all_start(lambda peer: face2_s.at[peer], face2_r, 4)
-    all_wait(lambda peer: face2_s.at[peer], face2_r, 4)
+    all_wait(face2_r, 4)
     reduced(face2_r, back2_s)
     back2_r[gy] = back2_s[gy]
     all_start(lambda peer: back2_s.at[peer], back2_r, 5)
-    all_wait(lambda peer: back2_s.at[peer], back2_r, 5)
+    all_wait(back2_r, 5)
     values = joined(local, back2_r)
     for y in range(rows):
         out[y] = values[y]
@@ -859,7 +924,8 @@
     part3 = three.rows // 4
     wide3 = wide2 // 2
     most = max(rows * wide, two.rows * two.wide, three.rows * three.wide)
-    scratch = [room(most, lanes), room(two.rows, two.wide, lanes)]
+    scratch = [pltpu.VMEM(arg.shape, arg.dtype) for arg in args]
+    scratch += [room(most, lanes), room(two.rows // 2, two.wide, lanes)]
     scratch += [room(rows, wide, lanes)] * 11
     scratch += [room(wide, lanes)] * 2
     scratch += [room(2, rows, lanes)] * 2 + [room(2, wide, lanes)] * 2
@@ -869,28 +935,29 @@
     scratch += [room(ngy, 6, share, lanes)] * 2 + [room(ngy, 2, share, lanes)] * 6
     scratch += [room(ngy, 3, share, lanes), room(ngy, 2, share, lanes)]
     scratch += [room(wide, lanes)] * 2
-    scratch += [room(2, rows, lanes)] * 4 + [room(2, two.rows, lanes)] * 4
+    scratch += [room(2, rows, lanes)] * 4 + [room(2, two.rows, lanes)] * 2
     scratch += [room(4, part3, wide3, lanes), room(ngx, 4, part3, wide3, lanes)]
     scratch += [room(part3, wide3, lanes), room(ngx, part3, wide3, lanes)]
     for level in levels:
         scratch += level.scratch()
     dma = pltpu.SemaphoreType.DMA
-    scratch += [dma((6, 2)), dma((6, 2)), dma((6, ngy)), dma((6, ngy)), dma((2, ngx)), dma((2, ngx))]
+    scratch += [dma((6, 2)), dma((6, 2)), dma((6,)), dma((6,)), dma((2, ngx)), dma((2, ngx)), dma((5,))]
+    scratch += [dma((ngy + 2,)), dma((ngy + 2,))]
     return pl.pallas_call(
         functools.partial(v_cycle_kernel, ngx, ngy, levels),
         out_shape=jax.ShapeDtypeStruct(args[0].shape, f32),
-        in_specs=[pl.BlockSpec(memory_space=pltpu.VMEM)] * 5,
+        in_specs=[pl.BlockSpec(memory_space=pltpu.HBM)] * 5,
         out_specs=pl.BlockSpec(memory_space=pltpu.VMEM),
         scratch_shapes=scratch,
         compiler_params=pltpu.CompilerParams(
-            collective_id=0, has_side_effects=True, vmem_limit_bytes=48 * 2**20
+            collective_id=0, has_side_effects=True, vmem_limit_bytes=63 * 2**20
         ),
     )(*args)
 
 
 def solution(mesh):
     ngx, ngy = mesh.shape["gx"], mesh.shape["gy"]
-    small = ngy <= 16 and ngx <= 4
+    small = ngy == 16 and ngx <= 4
     part = functools.partial(fused, ngx, ngy) if small else body
     return jax.shard_map(
         part,

time: 89.2 us -> 61.5 us (0.69)
  Pallas kernels: 83.9 us -> 59.8 us
  local copies, waits for them, and re-layouts: 5.18 us -> 1.57 us
    pallas_call x1, Pallas kernels: 83.9 us -> 59.8 us  [fused(): pl.pallas_call(functools.partial(v_cycle_kernel, ngx, ngy, levels), out_s...]
    unnamed x11 -> x1, local copies, waits for them, and re-layouts: 5.18 us -> 1.57 us
where the time goes in v2:
time: 61.5 us; the launch traced here: 61.4 us
  Pallas kernels  59.8 us (97%)
  local copies, waits for them, and re-layouts  1.57 us (3%)
    pallas_call x1, Pallas kernels, fused(): pl.pallas_call(functools.partial(v_cycle_kernel, ngx, ngy, levels), out_s...  59.8 us
    unnamed x1, local copies, waits for them, and re-layouts  1.57 us

profile of v2, /device:TPU:0, one launch (start us, length us, event | category | flops | bytes accessed | tf_op | source)
XLA Modules:
  0.0 61.4 jit_solution(17415406816028276971)
XLA Ops:
  0.0 59.8 %shard_map.55 = f32[8,32,128]{2,1,0:T(8,128)} custom-call(f32[8,32,128]{2,1,0:T(8,128)} %refs_0_.1, s32[8,32,128]{2,1,0:T(8,128)} %refs_1_.1, f32[8,32,128]{2,1,0:T(8,128)} %refs_2_.1, f32[8,32,128]{2,1,0:T(8,128)} %refs_3_.1, f32[8,32,128]{2,1,0:T(8,128)} %refs_4_.1), custom_call_target="tpu_custom_call" | custom-call | tf_op jit(solution)/shard_map/pallas_call | solution.py:946
  59.8 1.6 %copy.7 = f32[8,32,128]{2,1,0:T(8,128)} copy(f32[8,32,128]{2,1,0:T(8,128)} %shard_map.55) | data formatting | bytes 262144

commit v3 on v2

--- a/solution.py
+++ b/solution.py
@@ -439,15 +439,15 @@
             self.u[y] = value
             return value
 
-        looped(self.rows, down, zero, 8)
-        looped(self.rows, up, zero, 8)
+        looped(self.rows, down, zero, 16)
+        looped(self.rows, up, zero, 16)
 
     def residual(self, hold):
         def step(y, carry):
             hold[y] = self.beside(2 * y) + self.beside(2 * y + 1)
             return carry
 
-        looped(self.rows // 2, step, 0)
+        looped(self.rows // 2, step, 0, 8)
 
 
 def v_cycle_kernel(ngx, ngy, levels, *refs):
@@ -533,6 +533,8 @@
     place_c = lax.rem(gy, 2)
 
     def tree_slot(k):
+        if isinstance(k, int):
+            return (k % 2 * 2 + k // 2 % 2) * far_count + k // 4
         return (lax.rem(k, 2) * 2 + lax.rem(k // 2, 2)) * far_count + k // 4
 
     def tree_copies(stage):
@@ -689,8 +691,8 @@
             send[k, 1] = after
             return first
 
-        looped(ngy, down, zero)
-        looped(ngy, up, zero)
+        looped(ngy, down, zero, 16)
+        looped(ngy, up, zero, 16)
 
     def reduced_factor():
         def step(k, q):
@@ -701,7 +703,7 @@
             red[k, 2] = slope
             return face_r[k, 3] + face_r[k, 2] * q * slope
 
-        looped(ngy, step, jnp.zeros((share, lanes), jnp.float32))
+        looped(ngy, step, jnp.zeros((share, lanes), jnp.float32), 16)
 
     def joined(local, got):
         for owner in range(ngy):
@@ -787,7 +789,8 @@
             unpack2(target, lambda y: coef_r[tree_slot(k), place * quarter + y], k)
         return carry
 
-    lax.fori_loop(0, ngy, take_coefs, 0)
+    for k in range(ngy):
+        take_coefs(k, 0)
 
     rows3 = three.rows
     part3 = rows3 // 4
@@ -825,7 +828,8 @@
             h2_s[0, pl.ds(half * k + y, 1), :] = coef_r[tree_slot(k), 4 * quarter, pl.ds(y, 1), :]
         return carry
 
-    lax.fori_loop(0, ngy, take_edges, 0)
+    for k in range(ngy):
+        take_edges(k, 0)
     two.factor(edge2)
     all_wait(rhs_r, 3)
 
@@ -833,7 +837,8 @@
         unpack2(two.g, lambda y: rhs_r[k, y], k)
         return carry
 
-    lax.fori_loop(0, ngy, take_rhs, 0)
+    for k in range(ngy):
+        take_rhs(k, 0)
     two.solve(False)
 
     def outer_two(target):
@@ -842,7 +847,7 @@
             target[1, pl.ds(y, 1), :] = two.u[y, pl.ds(0, 1), :]
             return carry
 
-        looped(two.rows, step, 0)
+        looped(two.rows, step, 0, 16)
 
     outer_two(h2_s)
     beside_start(h2_s, h2_r, 3, 0)
@@ -881,7 +886,7 @@
             work[pl.ds(y, 1), :] = three.u[y, pl.ds(plane, 1), :]
             return carry
 
-        looped(rows3, pick, 0)
+        looped(rows3, pick, 0, 16)
         extra = times(work[pl.ds(0, rows3), :], spreading())
         work[pl.ds(0, rows3, stride=2), :] = extra
         work[pl.ds(1, rows3, stride=2), :] = extra

time: 61.5 us -> 58.9 us (0.958)
  Pallas kernels: 59.8 us -> 57.2 us
    pallas_call x1, Pallas kernels: 59.8 us -> 57.2 us  [fused(): pl.pallas_call(functools.partial(v_cycle_kernel, ngx, ngy, levels), out_s...]
where the time goes in v3:
time: 58.9 us; the launch traced here: 58.8 us
  Pallas kernels  57.2 us (97%)
  local copies, waits for them, and re-layouts  1.57 us (3%)
    pallas_call x1, Pallas kernels, fused(): pl.pallas_call(functools.partial(v_cycle_kernel, ngx, ngy, levels), out_s...  57.2 us
    unnamed x1, local copies, waits for them, and re-layouts  1.57 us

profile of v3, /device:TPU:0, one launch (start us, length us, event | category | flops | bytes accessed | tf_op | source)
XLA Modules:
  0.0 58.8 jit_solution(4159504257181084555)
XLA Ops:
  0.0 57.2 %shard_map.55 = f32[8,32,128]{2,1,0:T(8,128)} custom-call(f32[8,32,128]{2,1,0:T(8,128)} %refs_0_.1, s32[8,32,128]{2,1,0:T(8,128)} %refs_1_.1, f32[8,32,128]{2,1,0:T(8,128)} %refs_2_.1, f32[8,32,128]{2,1,0:T(8,128)} %refs_3_.1, f32[8,32,128]{2,1,0:T(8,128)} %refs_4_.1), custom_call_target="tpu_custom_call" | custom-call | tf_op jit(solution)/shard_map/pallas_call | solution.py:951
  57.2 1.6 %copy.7 = f32[8,32,128]{2,1,0:T(8,128)} copy(f32[8,32,128]{2,1,0:T(8,128)} %shard_map.55) | data formatting | bytes 262144
